TPU v7x, 256 devices: a whole 4x4x8 slice. The times are simulated.
256 devices in a mesh: pipe: 4 (over y), dp: 32 (over z, x), tensor: 2 (over core).
Axes of the slice: x: 4, y: 4, z: 8, core: 2. Of those that a mesh axis runs over, the one named last changes fastest.
Arguments:
- llm_grad: bfloat16 [4, 1024, 1664], P(None, 'dp'), may hold values from -6 to 6
- slot_row: int32 [4, 32, 32], P(None, 'dp'), may hold values from 0 to 31, each once within a row
- counts: int32 [32, 4], P('dp'), may hold values from 8 to 32, as said below
- saved_in: bfloat16 [4, 4, 1024, 1664], P('pipe', None, 'dp'), may hold values from -6 to 6
- saved_pre: bfloat16 [4, 4, 1024, 6400], P('pipe', None, 'dp', 'tensor'), may hold values from -6 to 6
- weights: bfloat16 [4, 1664, 6400], P('pipe', 'dp', 'tensor'), may hold values from -0.15625 to 0.15625
- channel_scale: float32 [4, 1664], P('pipe'), may hold values from 0.25 to 2
Outputs:
- weight_grad: bfloat16 [4, 1664, 6400], P('pipe', 'dp', 'tensor')
- section_grad: bfloat16 [4, 4, 1024, 1664], P('pipe', None, 'dp')
Inputs may be any that keep to these rules, and one draw needn't show every extreme that they name: For each micro-batch and rank, slot_row lists every row of the rank once. `counts`: both ends of the range occur in every draw.
All inputs are finite; a program needn't handle non-finite values.
Results may differ from a plain program's by a relative error of at most 0.023.
Values may be sent and summed in bfloat16 or wider, within the bound.
A program may use at most 128 MiB of HBM per device.

v0:
```python
import jax
import jax.numpy as jnp
from jax import lax
from jax.sharding import PartitionSpec as P

norm_eps = 1e-06
root_half = 0.7071067811865476
inv_root_two_pi = 0.3989422804014327


def shortened(value):

    def short(part):
        return part.astype(jnp.bfloat16) if part.dtype == jnp.float32 else part

    return jax.tree.map(short, value)


def shifted(block, axis, distance):
    devices = range(lax.axis_size(axis))
    route = [(i - distance, i) for i in devices if i - distance in devices]
    return lax.ppermute(block, axis, route)


def gelu_parts(pre_act):
    normal_cdf = 0.5 * (1.0 + jax.scipy.special.erf(pre_act * root_half))
    density = jnp.exp(-0.5 * pre_act * pre_act) * inv_root_two_pi
    return (pre_act * normal_cdf, normal_cdf + pre_act * density)


def local_top(llm_grad, slot_row, counts):
    row_count = llm_grad.shape[1]
    slot_ids = jnp.arange(row_count, dtype=jnp.int32)
    kept_mask = slot_ids[None, :] < counts[:, None]
    source = jnp.where(kept_mask[..., None], llm_grad, jnp.zeros_like(llm_grad))
    onehot = (slot_row[:, :, None] == slot_ids[None, None, :]).astype(jnp.bfloat16)
    placed = jnp.einsum("mjr,mjd->mrd", onehot, source, preferred_element_type=jnp.float32)
    return placed.astype(jnp.bfloat16)


def norm_back(incoming, dnorm, unit_rows, inv_std, channel_gain):
    scaled_back = dnorm * channel_gain
    back = inv_std * (
        scaled_back
        - jnp.mean(scaled_back, axis=-1, keepdims=True)
        - unit_rows * jnp.mean(scaled_back * unit_rows, axis=-1, keepdims=True)
    )
    return (incoming.astype(jnp.float32) + back).astype(jnp.bfloat16)


def add_term(grad_total, left_side, right_side):
    return grad_total + lax.dot_general(
        left_side, right_side, (((0,), (0,)), ((), ())), preferred_element_type=jnp.float32
    )


def keep_total(grad_total, left_side, right_side):
    return grad_total


def body(llm_grad, slot_row, counts, saved_in, saved_pre, weights, channel_scale):
    sections = lax.axis_size("pipe")
    section_index = lax.axis_index("pipe")
    micro_count = llm_grad.shape[0]
    row_count = llm_grad.shape[1]
    model_width = llm_grad.shape[2]
    hidden = saved_pre.shape[3]
    is_up = section_index % 2 == 0
    is_top = section_index == sections - 1
    full_weight = lax.all_gather(weights[0], "dp", axis=0, tiled=True)
    channel_gain = channel_scale[0]
    top_grad = local_top(llm_grad, slot_row[:, 0], counts[0])
    zero_wide = jnp.zeros((row_count, model_width), jnp.float32)
    zero_narrow = jnp.zeros((row_count, model_width), jnp.bfloat16)
    zero_hidden = jnp.zeros((row_count, hidden), jnp.bfloat16)

    def spare_work(incoming, hidden_in, inputs, pre_act):
        return (zero_wide, zero_hidden, zero_narrow, zero_hidden)

    def down_work(incoming, hidden_in, inputs, pre_act):
        scaled = (incoming.astype(jnp.float32) * channel_gain).astype(jnp.bfloat16)
        hidden_grad = jnp.dot(scaled, full_weight, preferred_element_type=jnp.float32).astype(
            jnp.bfloat16
        )
        activated = gelu_parts(pre_act.astype(jnp.float32))[0].astype(jnp.bfloat16)
        return (zero_wide, hidden_grad, scaled, activated)

    def up_work(incoming, hidden_in, inputs, pre_act):
        act_grad = (
            hidden_in.astype(jnp.float32) * gelu_parts(pre_act.astype(jnp.float32))[1]
        ).astype(jnp.bfloat16)
        values = inputs.astype(jnp.float32)
        center = values - jnp.mean(values, axis=-1, keepdims=True)
        inv_std = lax.rsqrt(jnp.mean(center * center, axis=-1, keepdims=True) + norm_eps)
        normed = (center * inv_std * channel_gain).astype(jnp.bfloat16)
        partial_value = lax.dot_general(
            act_grad, full_weight, (((1,), (1,)), ((), ())), preferred_element_type=jnp.float32
        )
        return (partial_value, zero_hidden, normed, act_grad)

    def advance(loop_state, tick_index):
        grad_store, out_buffer, recv_hidden, recv_res = loop_state
        micro_index = tick_index - (sections - 1 - section_index)
        is_valid = (micro_index >= 0) & (micro_index < micro_count)
        micro_safe = jnp.clip(micro_index, 0, micro_count - 1)
        incoming = jnp.where(is_top, top_grad[micro_safe], recv_res)
        inputs = saved_in[0, micro_safe]
        pre_act = saved_pre[0, micro_safe]
        branch = jnp.where(is_valid, jnp.where(is_up, 2, 1), 0).astype(jnp.int32)
        partial_value, hidden_out, left_side, right_side = lax.switch(
            branch, [spare_work, down_work, up_work], incoming, recv_hidden, inputs, pre_act
        )
        values = inputs.astype(jnp.float32)
        center = values - jnp.mean(values, axis=-1, keepdims=True)
        inv_std = lax.rsqrt(jnp.mean(center * center, axis=-1, keepdims=True) + norm_eps)
        unit_rows = center * inv_std
        summed = jax.tree.map(
            lambda part: part.astype(jnp.float32), lax.psum(shortened(partial_value), "tensor")
        )
        back_out = norm_back(incoming, summed, unit_rows, inv_std, channel_gain)
        outgoing = jnp.where(is_up, back_out, incoming)
        write_at = jnp.where(is_valid, micro_safe, micro_count)
        out_buffer = lax.dynamic_update_index_in_dim(out_buffer, outgoing, write_at, 0)
        grad_store = lax.cond(is_valid, add_term, keep_total, grad_store, left_side, right_side)
        recv_hidden, recv_res = (
            shifted(shortened(hidden_out), "pipe", -1).astype(hidden_out.dtype),
            shifted(outgoing, "pipe", -1),
        )
        return ((grad_store, out_buffer, recv_hidden, recv_res), None)

    grad_store = jnp.zeros((model_width, hidden), jnp.float32)
    out_buffer = jnp.zeros((micro_count + 1, row_count, model_width), jnp.bfloat16)
    tick_count = micro_count + sections - 1
    loop_state = (grad_store, out_buffer, zero_hidden, zero_narrow)
    loop_state, unused = lax.scan(advance, loop_state, jnp.arange(tick_count, dtype=jnp.int32))
    grad_store, out_buffer, recv_hidden, recv_res = loop_state
    weight_out = lax.psum_scatter(
        grad_store.astype(jnp.bfloat16), "dp", scatter_dimension=0, tiled=True
    )
    return (weight_out[None], out_buffer[:micro_count][None])


def solution(mesh):
    in_specs = (
        P(None, "dp", None),
        P(None, "dp", None),
        P("dp", None),
        P("pipe", None, "dp", None),
        P("pipe", None, "dp", "tensor"),
        P("pipe", "dp", "tensor"),
        P("pipe", None),
    )
    out_specs = (P("pipe", "dp", "tensor"), P("pipe", None, "dp", None))
    return jax.shard_map(body, mesh=mesh, in_specs=in_specs, out_specs=out_specs, check_vma=False)
```

profile of v0, /device:TPU:160, one launch (start us, length us, event | category | flops | bytes accessed | tf_op | source)
XLA Modules:
  0.0 917.6 jit_solution(5709121995667591268)
XLA Ops:
  7.2 2.4 copy.10
  10.3 1.4 convolution_convert_fusion.1
  11.7 160.9 %all-gather.3.cloned.1.call-done = bf16[1,1664,3200]{2,0,1:T(2,128)(2,1)} async-done(((bf16[1,52,3200]{2,0,1:T(2,128)(2,1)}), bf16[1,1664,3200]{2,0,1:T(2,128)(2,1)}) %all-gather.3.cloned.1.call-update) | async-done | bytes 10649616 | tf_op jit(solution)/shard_map/all_gather | solution.py:70
  172.6 15.3 %copy.13 = bf16[1,1664,3200]{2,1,0:T(8,128)(2,1)} copy(bf16[1,1664,3200]{2,0,1:T(2,128)(2,1)} %all-gather.3.cloned.1.call-done) | data formatting | bytes 21299200
  188.0 8.4 broadcast_in_dim.59
  196.5 443.6 %while.21 = (s32[]{:T(128)}, f32[1664,3200]{1,0:T(8,128)}, bf16[5,32,1664]{2,1,0:T(8,128)(2,1)S(1)}, bf16[32,3200]{1,0:T(8,128)(2,1)S(1)}, bf16[32,1664]{1,0:T(8...) while((s32[]{:T(128)}, f32[1664,3200]{1,0:T(8,128)}, ...), condition=%wide.region_13.14_spmd, body=%wide.region_0.13_spmd.sunk | while | flops 690257984 | bytes 59273832 | solution.py:135
  199.8 1.4 conditional.4
  201.9 1.3 collective-permute-start
  203.5 32.2 %all-reduce.4.cloned.1.call-done = bf16[32,1664]{1,0:T(8,128)(2,1)} async-done(((bf16[32,1664]{1,0:T(8,128)(2,1)}), bf16[32,1664]{1,0:T(8,128)(2,1)}) %all-reduce.4.cloned.1.call-update) | async-done | bytes 106512 | tf_op jit(solution)/shard_map/while/body/eval_jaxpr/psum | solution.py:118
  235.6 1.1 fusion.46
  237.8 1.3 collective-permute-start.1
  239.2 5.7 collective-permute-done.1
  248.2 1.4 conditional.4
  250.2 1.3 collective-permute-start
  251.8 47.5 %all-reduce.4.cloned.1.call-done = bf16[32,1664]{1,0:T(8,128)(2,1)} async-done(((bf16[32,1664]{1,0:T(8,128)(2,1)}), bf16[32,1664]{1,0:T(8,128)(2,1)}) %all-reduce.4.cloned.1.call-update) | async-done | bytes 106512 | tf_op jit(solution)/shard_map/while/body/eval_jaxpr/psum | solution.py:118
  299.2 1.1 fusion.46
  301.4 1.3 collective-permute-start.1
  302.8 5.7 collective-permute-done.1
  311.8 1.4 conditional.4
  313.9 1.3 collective-permute-start
  315.4 49.2 %all-reduce.4.cloned.1.call-done = bf16[32,1664]{1,0:T(8,128)(2,1)} async-done(((bf16[32,1664]{1,0:T(8,128)(2,1)}), bf16[32,1664]{1,0:T(8,128)(2,1)}) %all-reduce.4.cloned.1.call-update) | async-done | bytes 106512 | tf_op jit(solution)/shard_map/while/body/eval_jaxpr/psum | solution.py:118
  366.8 1.3 collective-permute-start.1
  368.1 5.7 collective-permute-done.1
  377.1 9.3 %conditional.4 = (bf16[32,1664]{1,0:T(8,128)(2,1)S(1)}, bf16[32,3200]{1,0:T(8,128)(2,1)S(1)}, bf16[32,1664]{1,0:T(8,128)(2,1)}, bf16[32,3200]{1,0:T(8,128)(2,1)}) conditional(s32[]{:T(128)} %clamp.6, () %tuple.65, (bf16[32,1664]{1,0:T(8,128)(2,1)S(1)}, f32[1,1664]{1,0:T(1,128)S(1)}, bf16[1664,3200]{1,0:T(8,128)(2,1)}, ...), branch_computations={%region_1.1_spmd, %region_2.2_spmd, %region_3.5_spmd} | conditional | flops 342601760 | bytes 12227238 | solution.py:110
  379.2 7.2 fusion.36
  387.2 1.3 collective-permute-start
  388.7 41.3 %all-reduce.4.cloned.1.call-done = bf16[32,1664]{1,0:T(8,128)(2,1)} async-done(((bf16[32,1664]{1,0:T(8,128)(2,1)}), bf16[32,1664]{1,0:T(8,128)(2,1)}) %all-reduce.4.cloned.1.call-update) | async-done | bytes 106512 | tf_op jit(solution)/shard_map/while/body/eval_jaxpr/psum | solution.py:118
  432.2 1.3 collective-permute-start.1
  433.5 17.3 %conditional.5 = (f32[1664,3200]{1,0:T(8,128)}) conditional(s32[]{:T(128)} %convert_element_type.179, f32[1664,3200]{1,0:T(8,128)} %get-tuple-element.404, (bf16[32,1664]{1,0:T(8,128)(2,1)}, bf16[32,3200]{1,0:T(8,128)(2,1)}, f32[1664,3200]{1,0:T(8,128)}) %tuple.68), branch_computations={%region_6.6_spmd, %region_7.7_spmd} | conditional | flops 346112000 | bytes 42909704 | solution.py:124
  433.5 17.3 %convolution_add_fusion = f32[1664,3200]{1,0:T(8,128)} fusion(f32[1664,3200]{1,0:T(8,128)} %get-tuple-element.188, bf16[32,1664]{1,0:T(8,128)(2,1)} %get-tuple-element.189, bf16[32,3200]{1,0:T(8,128)(2,1)} %get-tuple-element.190), kind=kOutput, calls=%fused_computation | convolution fusion | flops 346112000 | bytes 42909696 | tf_op jit(solution)/shard_map/while/body/eval_jaxpr/cond/branch_1_fun/dot_general | solution.py:52
  454.1 9.3 %conditional.4 = (bf16[32,1664]{1,0:T(8,128)(2,1)S(1)}, bf16[32,3200]{1,0:T(8,128)(2,1)S(1)}, bf16[32,1664]{1,0:T(8,128)(2,1)}, bf16[32,3200]{1,0:T(8,128)(2,1)}) conditional(s32[]{:T(128)} %clamp.6, () %tuple.65, (bf16[32,1664]{1,0:T(8,128)(2,1)S(1)}, f32[1,1664]{1,0:T(1,128)S(1)}, bf16[1664,3200]{1,0:T(8,128)(2,1)}, ...), branch_computations={%region_1.1_spmd, %region_2.2_spmd, %region_3.5_spmd} | conditional | flops 342601760 | bytes 12227238 | solution.py:110
  456.2 7.2 fusion.36
  464.1 1.3 collective-permute-start
  465.7 29.7 %all-reduce.4.cloned.1.call-done = bf16[32,1664]{1,0:T(8,128)(2,1)} async-done(((bf16[32,1664]{1,0:T(8,128)(2,1)}), bf16[32,1664]{1,0:T(8,128)(2,1)}) %all-reduce.4.cloned.1.call-update) | async-done | bytes 106512 | tf_op jit(solution)/shard_map/while/body/eval_jaxpr/psum | solution.py:118
  497.6 1.3 collective-permute-start.1
  498.9 17.3 %conditional.5 = (f32[1664,3200]{1,0:T(8,128)}) conditional(s32[]{:T(128)} %convert_element_type.179, f32[1664,3200]{1,0:T(8,128)} %get-tuple-element.404, (bf16[32,1664]{1,0:T(8,128)(2,1)}, bf16[32,3200]{1,0:T(8,128)(2,1)}, f32[1664,3200]{1,0:T(8,128)}) %tuple.68), branch_computations={%region_6.6_spmd, %region_7.7_spmd} | conditional | flops 346112000 | bytes 42909704 | solution.py:124
  498.9 17.3 %convolution_add_fusion = f32[1664,3200]{1,0:T(8,128)} fusion(f32[1664,3200]{1,0:T(8,128)} %get-tuple-element.188, bf16[32,1664]{1,0:T(8,128)(2,1)} %get-tuple-element.189, bf16[32,3200]{1,0:T(8,128)(2,1)} %get-tuple-element.190), kind=kOutput, calls=%fused_computation | convolution fusion | flops 346112000 | bytes 42909696 | tf_op jit(solution)/shard_map/while/body/eval_jaxpr/cond/branch_1_fun/dot_general | solution.py:52
  519.5 9.3 %conditional.4 = (bf16[32,1664]{1,0:T(8,128)(2,1)S(1)}, bf16[32,3200]{1,0:T(8,128)(2,1)S(1)}, bf16[32,1664]{1,0:T(8,128)(2,1)}, bf16[32,3200]{1,0:T(8,128)(2,1)}) conditional(s32[]{:T(128)} %clamp.6, () %tuple.65, (bf16[32,1664]{1,0:T(8,128)(2,1)S(1)}, f32[1,1664]{1,0:T(1,128)S(1)}, bf16[1664,3200]{1,0:T(8,128)(2,1)}, ...), branch_computations={%region_1.1_spmd, %region_2.2_spmd, %region_3.5_spmd} | conditional | flops 342601760 | bytes 12227238 | solution.py:110
  521.5 7.2 fusion.36
  529.5 1.3 collective-permute-start
  531.1 26.4 %all-reduce.4.cloned.1.call-done = bf16[32,1664]{1,0:T(8,128)(2,1)} async-done(((bf16[32,1664]{1,0:T(8,128)(2,1)}), bf16[32,1664]{1,0:T(8,128)(2,1)}) %all-reduce.4.cloned.1.call-update) | async-done | bytes 106512 | tf_op jit(solution)/shard_map/while/body/eval_jaxpr/psum | solution.py:118
  559.7 1.3 collective-permute-start.1
  561.0 17.3 %conditional.5 = (f32[1664,3200]{1,0:T(8,128)}) conditional(s32[]{:T(128)} %convert_element_type.179, f32[1664,3200]{1,0:T(8,128)} %get-tuple-element.404, (bf16[32,1664]{1,0:T(8,128)(2,1)}, bf16[32,3200]{1,0:T(8,128)(2,1)}, f32[1664,3200]{1,0:T(8,128)}) %tuple.68), branch_computations={%region_6.6_spmd, %region_7.7_spmd} | conditional | flops 346112000 | bytes 42909704 | solution.py:124
  561.0 17.3 %convolution_add_fusion = f32[1664,3200]{1,0:T(8,128)} fusion(f32[1664,3200]{1,0:T(8,128)} %get-tuple-element.188, bf16[32,1664]{1,0:T(8,128)(2,1)} %get-tuple-element.189, bf16[32,3200]{1,0:T(8,128)(2,1)} %get-tuple-element.190), kind=kOutput, calls=%fused_computation | convolution fusion | flops 346112000 | bytes 42909696 | tf_op jit(solution)/shard_map/while/body/eval_jaxpr/cond/branch_1_fun/dot_general | solution.py:52
  581.6 9.3 %conditional.4 = (bf16[32,1664]{1,0:T(8,128)(2,1)S(1)}, bf16[32,3200]{1,0:T(8,128)(2,1)S(1)}, bf16[32,1664]{1,0:T(8,128)(2,1)}, bf16[32,3200]{1,0:T(8,128)(2,1)}) conditional(s32[]{:T(128)} %clamp.6, () %tuple.65, (bf16[32,1664]{1,0:T(8,128)(2,1)S(1)}, f32[1,1664]{1,0:T(1,128)S(1)}, bf16[1664,3200]{1,0:T(8,128)(2,1)}, ...), branch_computations={%region_1.1_spmd, %region_2.2_spmd, %region_3.5_spmd} | conditional | flops 342601760 | bytes 12227238 | solution.py:110
  583.6 7.2 fusion.36
  591.6 1.3 collective-permute-start
  593.1 26.1 %all-reduce.4.cloned.1.call-done = bf16[32,1664]{1,0:T(8,128)(2,1)} async-done(((bf16[32,1664]{1,0:T(8,128)(2,1)}), bf16[32,1664]{1,0:T(8,128)(2,1)}) %all-reduce.4.cloned.1.call-update) | async-done | bytes 106512 | tf_op jit(solution)/shard_map/while/body/eval_jaxpr/psum | solution.py:118
  621.4 1.3 collective-permute-start.1
  622.7 17.3 %conditional.5 = (f32[1664,3200]{1,0:T(8,128)}) conditional(s32[]{:T(128)} %convert_element_type.179, f32[1664,3200]{1,0:T(8,128)} %get-tuple-element.404, (bf16[32,1664]{1,0:T(8,128)(2,1)}, bf16[32,3200]{1,0:T(8,128)(2,1)}, f32[1664,3200]{1,0:T(8,128)}) %tuple.68), branch_computations={%region_6.6_spmd, %region_7.7_spmd} | conditional | flops 346112000 | bytes 42909704 | solution.py:124
  622.8 17.3 %convolution_add_fusion = f32[1664,3200]{1,0:T(8,128)} fusion(f32[1664,3200]{1,0:T(8,128)} %get-tuple-element.188, bf16[32,1664]{1,0:T(8,128)(2,1)} %get-tuple-element.189, bf16[32,3200]{1,0:T(8,128)(2,1)} %get-tuple-element.190), kind=kOutput, calls=%fused_computation | convolution fusion | flops 346112000 | bytes 42909696 | tf_op jit(solution)/shard_map/while/body/eval_jaxpr/cond/branch_1_fun/dot_general | solution.py:52
  640.1 12.3 %convert_element_type.68 = bf16[1664,3200]{1,0:T(8,128)(2,1)} convert(f32[1664,3200]{1,0:T(8,128)} %get-tuple-element.215) | non-fusion elementwise | flops 5324800 | bytes 31948800 | tf_op jit(solution)/shard_map/convert_element_type | solution.py:138
  652.4 150.3 %fusion = bf16[64,3200]{1,0:T(8,128)(2,1)S(1)} fusion(bf16[1664,3200]{1,0:T(8,128)(2,1)} %convert_element_type.68), kind=kCustom, calls=%all-reduce-scatter | all-reduce-scatter fusion | flops 6553601 | bytes 11060224
  802.8 2.0 collective-permute-start.7
  806.0 1.9 collective-permute-start.2
  807.9 5.7 collective-permute-start.3
  813.7 1.9 collective-permute-start.4
  815.6 1.9 collective-permute-start.5
  817.5 11.5 %collective-permute-done.7 = bf16[52,3200]{1,0:T(8,128)(2,1)S(1)} collective-permute-done((bf16[52,3200]{1,0:T(8,128)(2,1)S(1)}, bf16[52,3200]{1,0:T(8,128)(2,1)S(1)}, u32[]{:S(2)}, u32[]{:S(2)}) %collective-permute-start.7) | collective-permute-done | bytes 332832
  829.0 1.9 collective-permute-start.6
  831.7 7.9 collective-permute-done.2
  839.6 1.4 collective-permute-done.3
  842.7 46.2 %collective-permute-done.6 = bf16[64,3200]{1,0:T(8,128)(2,1)} collective-permute-done((bf16[64,3200]{1,0:T(8,128)(2,1)S(1)}, bf16[64,3200]{1,0:T(8,128)(2,1)}, u32[]{:S(2)}, u32[]{:S(2)}) %collective-permute-start.6) | collective-permute-done | bytes 409632
  888.8 21.1 %concatenate = bf16[436,3200]{1,0:T(8,128)(2,1)S(1)} concatenate(bf16[52,3200]{1,0:T(8,128)(2,1)} %copy-done.6, bf16[64,3200]{1,0:T(8,128)(2,1)} %collective-permute-done.6, bf16[64,3200]{1,0:T(8,128)(2,1)} %copy-done.5, bf16[64,3200]{1,0:T(8,128)(2,1)} %copy-done.4, bf16[64,3200]{1,0:T(8,128)(2,1)} %copy-done.3, bf16[64,3200]{1,0:T(8,128)(2,1)} %copy-done.2, ...), dimensions={0} | concatenate | bytes 5580800
  (188 shorter events, 54.7 us)
Async XLA Ops:
  7.2 165.5 %all-gather.3.cloned.1.call-start = ((), (), s32[]{:S(2)}) async-start(), calls=%async_computation | async-start | bytes 21964800 | tf_op jit(solution)/shard_map/all_gather | solution.py:70
  188.0 8.5 copy-start.1
  196.5 39.1 %all-reduce.4.cloned.1.call-start = ((), (), s32[]{:S(2)}) async-start(), calls=%async_computation.1 | async-start | bytes 212992 | tf_op jit(solution)/shard_map/while/body/eval_jaxpr/psum | solution.py:118
  201.2 0.7 copy-start
  201.9 37.2 %collective-permute-start = (bf16[32,3200]{1,0:T(8,128)(2,1)S(1)}, bf16[32,3200]{1,0:T(8,128)(2,1)S(1)}, u32[]{:S(2)}, u32[]{:S(2)}) collective-permute-start(bf16[32,3200]{1,0:T(8,128)(2,1)S(1)} %get-tuple-element.368), channel_id=1, source_target_pairs={{64,0},{128,64},{192,128},{65,1},{129,65},{193,129},{66,2},{130,66... | collective-permute-start | bytes 614408 | tf_op jit(solution)/shard_map/while/body/eval_jaxpr/ppermute | solution.py:22
  237.8 7.1 collective-permute-start.1
  244.9 54.4 %all-reduce.4.cloned.1.call-start = ((), (), s32[]{:S(2)}) async-start(), calls=%async_computation.1 | async-start | bytes 212992 | tf_op jit(solution)/shard_map/while/body/eval_jaxpr/psum | solution.py:118
  249.6 0.7 copy-start
  250.2 52.5 %collective-permute-start = (bf16[32,3200]{1,0:T(8,128)(2,1)S(1)}, bf16[32,3200]{1,0:T(8,128)(2,1)S(1)}, u32[]{:S(2)}, u32[]{:S(2)}) collective-permute-start(bf16[32,3200]{1,0:T(8,128)(2,1)S(1)} %get-tuple-element.368), channel_id=1, source_target_pairs={{64,0},{128,64},{192,128},{65,1},{129,65},{193,129},{66,2},{130,66... | collective-permute-start | bytes 614408 | tf_op jit(solution)/shard_map/while/body/eval_jaxpr/ppermute | solution.py:22
  301.4 7.1 collective-permute-start.1
  308.5 56.1 %all-reduce.4.cloned.1.call-start = ((), (), s32[]{:S(2)}) async-start(), calls=%async_computation.1 | async-start | bytes 212992 | tf_op jit(solution)/shard_map/while/body/eval_jaxpr/psum | solution.py:118
  313.2 0.7 copy-start
  313.9 54.3 %collective-permute-start = (bf16[32,3200]{1,0:T(8,128)(2,1)S(1)}, bf16[32,3200]{1,0:T(8,128)(2,1)S(1)}, u32[]{:S(2)}, u32[]{:S(2)}) collective-permute-start(bf16[32,3200]{1,0:T(8,128)(2,1)S(1)} %get-tuple-element.368), channel_id=1, source_target_pairs={{64,0},{128,64},{192,128},{65,1},{129,65},{193,129},{66,2},{130,66... | collective-permute-start | bytes 614408 | tf_op jit(solution)/shard_map/while/body/eval_jaxpr/ppermute | solution.py:22
  366.8 7.1 collective-permute-start.1
  373.9 56.1 %all-reduce.4.cloned.1.call-start = ((), (), s32[]{:S(2)}) async-start(), calls=%async_computation.1 | async-start | bytes 212992 | tf_op jit(solution)/shard_map/while/body/eval_jaxpr/psum | solution.py:118
  386.5 0.7 copy-start
  387.2 63.6 %collective-permute-start = (bf16[32,3200]{1,0:T(8,128)(2,1)S(1)}, bf16[32,3200]{1,0:T(8,128)(2,1)S(1)}, u32[]{:S(2)}, u32[]{:S(2)}) collective-permute-start(bf16[32,3200]{1,0:T(8,128)(2,1)S(1)} %get-tuple-element.368), channel_id=1, source_target_pairs={{64,0},{128,64},{192,128},{65,1},{129,65},{193,129},{66,2},{130,66... | collective-permute-start | bytes 614408 | tf_op jit(solution)/shard_map/while/body/eval_jaxpr/ppermute | solution.py:22
  432.2 18.6 %collective-permute-start.1 = (bf16[32,1664]{1,0:T(8,128)(2,1)S(1)}, bf16[32,1664]{1,0:T(8,128)(2,1)S(1)}, u32[]{:S(2)}, u32[]{:S(2)}) collective-permute-start(bf16[32,1664]{1,0:T(8,128)(2,1)S(1)} %get-tuple-element.369), channel_id=1, source_target_pairs={{64,0},{128,64},{192,128},{65,1},{129,65},{193,129},{66,2},{130,66... | collective-permute-start | bytes 319496 | tf_op jit(solution)/shard_map/while/body/eval_jaxpr/ppermute | solution.py:22
  450.8 44.6 %all-reduce.4.cloned.1.call-start = ((), (), s32[]{:S(2)}) async-start(), calls=%async_computation.1 | async-start | bytes 212992 | tf_op jit(solution)/shard_map/while/body/eval_jaxpr/psum | solution.py:118
  463.5 0.7 copy-start
  464.1 52.1 %collective-permute-start = (bf16[32,3200]{1,0:T(8,128)(2,1)S(1)}, bf16[32,3200]{1,0:T(8,128)(2,1)S(1)}, u32[]{:S(2)}, u32[]{:S(2)}) collective-permute-start(bf16[32,3200]{1,0:T(8,128)(2,1)S(1)} %get-tuple-element.368), channel_id=1, source_target_pairs={{64,0},{128,64},{192,128},{65,1},{129,65},{193,129},{66,2},{130,66... | collective-permute-start | bytes 614408 | tf_op jit(solution)/shard_map/while/body/eval_jaxpr/ppermute | solution.py:22
  497.6 18.6 %collective-permute-start.1 = (bf16[32,1664]{1,0:T(8,128)(2,1)S(1)}, bf16[32,1664]{1,0:T(8,128)(2,1)S(1)}, u32[]{:S(2)}, u32[]{:S(2)}) collective-permute-start(bf16[32,1664]{1,0:T(8,128)(2,1)S(1)} %get-tuple-element.369), channel_id=1, source_target_pairs={{64,0},{128,64},{192,128},{65,1},{129,65},{193,129},{66,2},{130,66... | collective-permute-start | bytes 319496 | tf_op jit(solution)/shard_map/while/body/eval_jaxpr/ppermute | solution.py:22
  516.2 41.3 %all-reduce.4.cloned.1.call-start = ((), (), s32[]{:S(2)}) async-start(), calls=%async_computation.1 | async-start | bytes 212992 | tf_op jit(solution)/shard_map/while/body/eval_jaxpr/psum | solution.py:118
  528.8 0.7 copy-start
  529.5 48.7 %collective-permute-start = (bf16[32,3200]{1,0:T(8,128)(2,1)S(1)}, bf16[32,3200]{1,0:T(8,128)(2,1)S(1)}, u32[]{:S(2)}, u32[]{:S(2)}) collective-permute-start(bf16[32,3200]{1,0:T(8,128)(2,1)S(1)} %get-tuple-element.368), channel_id=1, source_target_pairs={{64,0},{128,64},{192,128},{65,1},{129,65},{193,129},{66,2},{130,66... | collective-permute-start | bytes 614408 | tf_op jit(solution)/shard_map/while/body/eval_jaxpr/ppermute | solution.py:22
  559.7 18.6 %collective-permute-start.1 = (bf16[32,1664]{1,0:T(8,128)(2,1)S(1)}, bf16[32,1664]{1,0:T(8,128)(2,1)S(1)}, u32[]{:S(2)}, u32[]{:S(2)}) collective-permute-start(bf16[32,1664]{1,0:T(8,128)(2,1)S(1)} %get-tuple-element.369), channel_id=1, source_target_pairs={{64,0},{128,64},{192,128},{65,1},{129,65},{193,129},{66,2},{130,66... | collective-permute-start | bytes 319496 | tf_op jit(solution)/shard_map/while/body/eval_jaxpr/ppermute | solution.py:22
  578.3 41.0 %all-reduce.4.cloned.1.call-start = ((), (), s32[]{:S(2)}) async-start(), calls=%async_computation.1 | async-start | bytes 212992 | tf_op jit(solution)/shard_map/while/body/eval_jaxpr/psum | solution.py:118
  590.9 0.7 copy-start
  591.6 48.5 %collective-permute-start = (bf16[32,3200]{1,0:T(8,128)(2,1)S(1)}, bf16[32,3200]{1,0:T(8,128)(2,1)S(1)}, u32[]{:S(2)}, u32[]{:S(2)}) collective-permute-start(bf16[32,3200]{1,0:T(8,128)(2,1)S(1)} %get-tuple-element.368), channel_id=1, source_target_pairs={{64,0},{128,64},{192,128},{65,1},{129,65},{193,129},{66,2},{130,66... | collective-permute-start | bytes 614408 | tf_op jit(solution)/shard_map/while/body/eval_jaxpr/ppermute | solution.py:22
  621.4 18.6 %collective-permute-start.1 = (bf16[32,1664]{1,0:T(8,128)(2,1)S(1)}, bf16[32,1664]{1,0:T(8,128)(2,1)S(1)}, u32[]{:S(2)}, u32[]{:S(2)}) collective-permute-start(bf16[32,1664]{1,0:T(8,128)(2,1)S(1)} %get-tuple-element.369), channel_id=1, source_target_pairs={{64,0},{128,64},{192,128},{65,1},{129,65},{193,129},{66,2},{130,66... | collective-permute-start | bytes 319496 | tf_op jit(solution)/shard_map/while/body/eval_jaxpr/ppermute | solution.py:22
  640.1 164.7 %copy-start.7 = (u32[256]{0:T(256)S(1)}, u32[256]{0:T(256)}, u32[]{:S(2)}) copy-start(u32[256]{0:T(256)} %constant.123) | copy-start | bytes 3076
  802.8 26.2 %collective-permute-start.7 = (bf16[52,3200]{1,0:T(8,128)(2,1)S(1)}, bf16[52,3200]{1,0:T(8,128)(2,1)S(1)}, u32[]{:S(2)}, u32[]{:S(2)}) collective-permute-start(bf16[52,3200]{1,0:T(8,128)(2,1)S(1)} %slice.4), channel_id=1, source_target_pairs={{0,12},{2,14},{4,16},{6,18},{8,20},{10,22},{12,24},{14,26},{16,28}... | collective-permute-start | bytes 998408
  806.0 33.6 %collective-permute-start.2 = (bf16[64,3200]{1,0:T(8,128)(2,1)S(1)}, bf16[64,3200]{1,0:T(8,128)(2,1)S(1)}, u32[]{:S(2)}, u32[]{:S(2)}) collective-permute-start(bf16[64,3200]{1,0:T(8,128)(2,1)S(1)} %fusion), channel_id=1, source_target_pairs={{0,2},{2,4},{4,6},{6,8},{8,10},{10,12},{12,14},{14,16},{16,18},{18... | collective-permute-start | bytes 1228808
  807.9 33.1 %collective-permute-start.3 = (bf16[64,3200]{1,0:T(8,128)(2,1)S(1)}, bf16[64,3200]{1,0:T(8,128)(2,1)S(1)}, u32[]{:S(2)}, u32[]{:S(2)}) collective-permute-start(bf16[64,3200]{1,0:T(8,128)(2,1)S(1)} %fusion), channel_id=1, source_target_pairs={{0,4},{2,6},{4,8},{6,10},{8,12},{10,14},{12,16},{14,18},{16,20},{1... | collective-permute-start | bytes 1228808
  813.7 27.3 %collective-permute-start.4 = (bf16[64,3200]{1,0:T(8,128)(2,1)S(1)}, bf16[64,3200]{1,0:T(8,128)(2,1)S(1)}, u32[]{:S(2)}, u32[]{:S(2)}) collective-permute-start(bf16[64,3200]{1,0:T(8,128)(2,1)S(1)} %fusion), channel_id=1, source_target_pairs={{0,6},{2,8},{4,10},{6,12},{8,14},{10,16},{12,18},{14,20},{16,22},{... | collective-permute-start | bytes 1228808
  815.6 25.4 %collective-permute-start.5 = (bf16[64,3200]{1,0:T(8,128)(2,1)S(1)}, bf16[64,3200]{1,0:T(8,128)(2,1)S(1)}, u32[]{:S(2)}, u32[]{:S(2)}) collective-permute-start(bf16[64,3200]{1,0:T(8,128)(2,1)S(1)} %fusion), channel_id=1, source_target_pairs={{0,8},{2,10},{4,12},{6,14},{8,16},{10,18},{12,20},{14,22},{16,24},... | collective-permute-start | bytes 1228808
  829.0 12.0 %copy-start.6 = (bf16[52,3200]{1,0:T(8,128)(2,1)}, bf16[52,3200]{1,0:T(8,128)(2,1)S(1)}, u32[]{:S(2)}) copy-start(bf16[52,3200]{1,0:T(8,128)(2,1)S(1)} %collective-permute-done.7) | copy-start | bytes 998404
  829.0 59.8 %collective-permute-start.6 = (bf16[64,3200]{1,0:T(8,128)(2,1)S(1)}, bf16[64,3200]{1,0:T(8,128)(2,1)}, u32[]{:S(2)}, u32[]{:S(2)}) collective-permute-start(bf16[64,3200]{1,0:T(8,128)(2,1)S(1)} %fusion), channel_id=1, source_target_pairs={{0,10},{2,12},{4,14},{6,16},{8,18},{10,20},{12,22},{14,24},{16,26}... | collective-permute-start | bytes 1228808
  839.6 1.4 copy-start.2
  841.0 0.8 copy-start.3
  841.0 0.9 copy-start.4
  841.9 0.7 copy-start.5
Sparse Core Ops, SparseCore 0:
  10.6 161.9 all-gather.2
  202.0 33.5 all-reduce.3
  250.4 48.8 all-reduce.3
  314.0 50.5 all-reduce.3
  387.3 42.6 all-reduce.3
  464.3 31.0 all-reduce.3
  529.6 27.7 all-reduce.3
  591.7 27.4 all-reduce.3
where the time goes:
time: 920 us; the launch traced here: 918 us
  waiting for transfers between devices  498 us (54%)
  blocking collectives  150 us (16%)
  matrix products  99.5 us (11%)
  local copies, waits for them, and re-layouts  70.8 us (8%)
  other arithmetic  45.2 us (5%)
  starting transfers between devices  33.6 us (4%)
  between operations  14.8 us (2%)
    psum x7, waiting for transfers between devices, advance(): lax.psum(shortened(partial_value), 'tensor')  252 us
    all_gather x1, waiting for transfers between devices, body(): full_weight = lax.all_gather(weights[0], 'dp', axis=0, tiled=True)  161 us
    unnamed x1, blocking collectives  150 us
    dot_general x4, matrix products, add_term(): lax.dot_general(left_side, right_side, (((0,), (0,)), ((), ())), preferre...  69.1 us
    unnamed x7, waiting for transfers between devices  66.9 us
    unnamed x19, local copies, waits for them, and re-layouts  41.1 us
    dot_general x4, matrix products, up_work(): lax.dot_general(act_grad, full_weight, (((1,), (1,)), ((), ())), preferre...  29 us
  transfers between devices with their start and end apart: 28, of which 15 were waited for; matrix products, arithmetic and copies ran while one was open for 10% of the time, Pallas kernels for 0%

commit v1 on v0

--- a/solution.py
+++ b/solution.py
@@ -67,7 +67,9 @@
     hidden = saved_pre.shape[3]
     is_up = section_index % 2 == 0
     is_top = section_index == sections - 1
-    full_weight = lax.all_gather(weights[0], "dp", axis=0, tiled=True)
+    full_weight = jnp.concatenate(
+        lax.all_to_all(jnp.stack([weights[0]] * lax.axis_size("dp")), "dp", 0, 0), axis=0
+    )
     channel_gain = channel_scale[0]
     top_grad = local_top(llm_grad, slot_row[:, 0], counts[0])
     zero_wide = jnp.zeros((row_count, model_width), jnp.float32)

time: 920 us -> 1040 us (1.13)
  waiting for transfers between devices: 498 us -> 607 us
    all_to_all x0 -> x1, waiting for transfers between devices: none -> 263 us  [body(): lax.all_to_all(jnp.stack([weights[0]] * lax.axis_size('dp')), 'dp', 0, 0)]
    all_gather x1 -> x0, waiting for transfers between devices: 161 us -> none  [body(): full_weight = lax.all_gather(weights[0], 'dp', axis=0, tiled=True)]
    unnamed x19 -> x23, local copies, waits for them, and re-layouts: 41.1 us -> 23.4 us
    reshape x0 -> x1, local copies, waits for them, and re-layouts: none -> 13.9 us  [body(): jnp.concatenate(lax.all_to_all(jnp.stack([weights[0]] * lax.axis_size('dp...]
    unnamed x7 -> x6, waiting for transfers between devices: 66.9 us -> 66.9 us
  transfers between devices with their start and end apart: 28 -> 28, of which waited for: 15 -> 15; matrix products, arithmetic and copies ran while one was open for 10% -> 8% of each run, Pallas kernels for 0% -> 0%
where the time goes in v1:
time: 1040 us
  waiting for transfers between devices  607 us (58%)
  blocking collectives  150 us (14%)
  matrix products  98.4 us (9%)
  local copies, waits for them, and re-layouts  72.9 us (7%)
  other arithmetic  44.5 us (4%)
  starting transfers between devices  43.2 us (4%)
  between operations  14.8 us (1%)
    all_to_all x1, waiting for transfers between devices, body(): lax.all_to_all(jnp.stack([weights[0]] * lax.axis_size('dp')), 'dp', 0, 0)  263 us
    psum x7, waiting for transfers between devices, advance(): lax.psum(shortened(partial_value), 'tensor')  260 us
    unnamed x1, blocking collectives  150 us
    dot_general x4, matrix products, add_term(): lax.dot_general(left_side, right_side, (((0,), (0,)), ((), ())), preferre...  69.2 us
    unnamed x6, waiting for transfers between devices  66.9 us
    dot_general x4, matrix products, up_work(): lax.dot_general(act_grad, full_weight, (((1,), (1,)), ((), ())), preferre...  29 us
    unnamed x23, local copies, waits for them, and re-layouts  23.4 us
  transfers between devices with their start and end apart: 28, of which 15 were waited for; matrix products, arithmetic and copies ran while one was open for 8% of the time, Pallas kernels for 0%

profile of v1, /device:TPU:160, one launch (start us, length us, event | category | flops | bytes accessed | tf_op | source)
XLA Modules:
  0.0 1037.5 jit_solution(8685593403046089057)
XLA Ops:
  7.2 5.9 stack.3
  13.1 9.6 all-to-all-start
  23.1 263.4 %all-to-all-done = bf16[32,52,3200]{2,1,0:T(8,128)(2,1)} async-done(((bf16[32,52,3200]{2,1,0:T(8,128)(2,1)}), bf16[32,52,3200]{2,1,0:T(8,128)(2,1)}, u32[]{:S(2)}, u32[]{:S(2)}) %all-to-all-start) | async-done | bytes 10649632 | tf_op jit(solution)/shard_map/all_to_all | solution.py:71
  286.5 13.9 %reshape.69 = bf16[1664,3200]{1,0:T(8,128)(2,1)} reshape(bf16[32,52,3200]{2,1,0:T(8,128)(2,1)} %all-to-all-done) | data formatting | bytes 21299200 | tf_op jit(solution)/shard_map/reshape | solution.py:70
  300.4 8.4 broadcast_in_dim.59
  309.0 450.9 %while.21 = (s32[]{:T(128)}, f32[1664,3200]{1,0:T(8,128)}, bf16[5,32,1664]{2,1,0:T(8,128)(2,1)S(1)}, bf16[32,3200]{1,0:T(8,128)(2,1)S(1)}, bf16[32,1664]{1,0:T(8...) while((s32[]{:T(128)}, f32[1664,3200]{1,0:T(8,128)}, ...), condition=%wide.region_13.14_spmd, body=%wide.region_0.13_spmd.sunk | while | flops 690257984 | bytes 59273832 | solution.py:137
  312.3 1.4 conditional.4
  314.4 1.3 collective-permute-start
  315.9 39.5 %all-reduce.4.cloned.1.call-done = bf16[32,1664]{1,0:T(8,128)(2,1)} async-done(((bf16[32,1664]{1,0:T(8,128)(2,1)}), bf16[32,1664]{1,0:T(8,128)(2,1)}) %all-reduce.4.cloned.1.call-update) | async-done | bytes 106512 | tf_op jit(solution)/shard_map/while/body/eval_jaxpr/psum | solution.py:120
  355.4 1.1 fusion.46
  357.6 1.3 collective-permute-start.1
  359.0 5.7 collective-permute-done.1
  368.0 1.4 conditional.4
  370.0 1.3 collective-permute-start
  371.6 47.5 %all-reduce.4.cloned.1.call-done = bf16[32,1664]{1,0:T(8,128)(2,1)} async-done(((bf16[32,1664]{1,0:T(8,128)(2,1)}), bf16[32,1664]{1,0:T(8,128)(2,1)}) %all-reduce.4.cloned.1.call-update) | async-done | bytes 106512 | tf_op jit(solution)/shard_map/while/body/eval_jaxpr/psum | solution.py:120
  419.0 1.1 fusion.46
  421.2 1.3 collective-permute-start.1
  422.6 5.7 collective-permute-done.1
  431.6 1.4 conditional.4
  433.6 1.3 collective-permute-start
  435.2 49.2 %all-reduce.4.cloned.1.call-done = bf16[32,1664]{1,0:T(8,128)(2,1)} async-done(((bf16[32,1664]{1,0:T(8,128)(2,1)}), bf16[32,1664]{1,0:T(8,128)(2,1)}) %all-reduce.4.cloned.1.call-update) | async-done | bytes 106512 | tf_op jit(solution)/shard_map/while/body/eval_jaxpr/psum | solution.py:120
  486.6 1.3 collective-permute-start.1
  488.0 5.7 collective-permute-done.1
  497.0 9.3 conditional.4
  499.0 7.2 fusion.36
  507.0 1.3 collective-permute-start
  508.5 41.3 %all-reduce.4.cloned.1.call-done = bf16[32,1664]{1,0:T(8,128)(2,1)} async-done(((bf16[32,1664]{1,0:T(8,128)(2,1)}), bf16[32,1664]{1,0:T(8,128)(2,1)}) %all-reduce.4.cloned.1.call-update) | async-done | bytes 106512 | tf_op jit(solution)/shard_map/while/body/eval_jaxpr/psum | solution.py:120
  552.0 1.3 collective-permute-start.1
  553.3 17.3 %conditional.5 = (f32[1664,3200]{1,0:T(8,128)}) conditional(s32[]{:T(128)} %convert_element_type.179, f32[1664,3200]{1,0:T(8,128)} %get-tuple-element.404, (bf16[32,1664]{1,0:T(8,128)(2,1)}, bf16[32,3200]{1,0:T(8,128)(2,1)}, f32[1664,3200]{1,0:T(8,128)}) %tuple.68), branch_computations={%region_6.6_spmd, %region_7.7_spmd} | conditional | flops 346112000 | bytes 42909704 | solution.py:126
  553.3 17.3 %convolution_add_fusion = f32[1664,3200]{1,0:T(8,128)} fusion(f32[1664,3200]{1,0:T(8,128)} %get-tuple-element.188, bf16[32,1664]{1,0:T(8,128)(2,1)} %get-tuple-element.189, bf16[32,3200]{1,0:T(8,128)(2,1)} %get-tuple-element.190), kind=kOutput, calls=%fused_computation | convolution fusion | flops 346112000 | bytes 42909696 | tf_op jit(solution)/shard_map/while/body/eval_jaxpr/cond/branch_1_fun/dot_general | solution.py:52
  573.9 9.3 conditional.4
  576.0 7.2 fusion.36
  583.9 1.3 collective-permute-start
  585.5 29.7 %all-reduce.4.cloned.1.call-done = bf16[32,1664]{1,0:T(8,128)(2,1)} async-done(((bf16[32,1664]{1,0:T(8,128)(2,1)}), bf16[32,1664]{1,0:T(8,128)(2,1)}) %all-reduce.4.cloned.1.call-update) | async-done | bytes 106512 | tf_op jit(solution)/shard_map/while/body/eval_jaxpr/psum | solution.py:120
  617.4 1.3 collective-permute-start.1
  618.7 17.3 %conditional.5 = (f32[1664,3200]{1,0:T(8,128)}) conditional(s32[]{:T(128)} %convert_element_type.179, f32[1664,3200]{1,0:T(8,128)} %get-tuple-element.404, (bf16[32,1664]{1,0:T(8,128)(2,1)}, bf16[32,3200]{1,0:T(8,128)(2,1)}, f32[1664,3200]{1,0:T(8,128)}) %tuple.68), branch_computations={%region_6.6_spmd, %region_7.7_spmd} | conditional | flops 346112000 | bytes 42909704 | solution.py:126
  618.7 17.3 %convolution_add_fusion = f32[1664,3200]{1,0:T(8,128)} fusion(f32[1664,3200]{1,0:T(8,128)} %get-tuple-element.188, bf16[32,1664]{1,0:T(8,128)(2,1)} %get-tuple-element.189, bf16[32,3200]{1,0:T(8,128)(2,1)} %get-tuple-element.190), kind=kOutput, calls=%fused_computation | convolution fusion | flops 346112000 | bytes 42909696 | tf_op jit(solution)/shard_map/while/body/eval_jaxpr/cond/branch_1_fun/dot_general | solution.py:52
  639.3 9.3 conditional.4
  641.4 7.2 fusion.36
  649.3 1.3 collective-permute-start
  650.9 26.4 %all-reduce.4.cloned.1.call-done = bf16[32,1664]{1,0:T(8,128)(2,1)} async-done(((bf16[32,1664]{1,0:T(8,128)(2,1)}), bf16[32,1664]{1,0:T(8,128)(2,1)}) %all-reduce.4.cloned.1.call-update) | async-done | bytes 106512 | tf_op jit(solution)/shard_map/while/body/eval_jaxpr/psum | solution.py:120
  679.5 1.3 collective-permute-start.1
  680.8 17.3 %conditional.5 = (f32[1664,3200]{1,0:T(8,128)}) conditional(s32[]{:T(128)} %convert_element_type.179, f32[1664,3200]{1,0:T(8,128)} %get-tuple-element.404, (bf16[32,1664]{1,0:T(8,128)(2,1)}, bf16[32,3200]{1,0:T(8,128)(2,1)}, f32[1664,3200]{1,0:T(8,128)}) %tuple.68), branch_computations={%region_6.6_spmd, %region_7.7_spmd} | conditional | flops 346112000 | bytes 42909704 | solution.py:126
  680.8 17.3 %convolution_add_fusion = f32[1664,3200]{1,0:T(8,128)} fusion(f32[1664,3200]{1,0:T(8,128)} %get-tuple-element.188, bf16[32,1664]{1,0:T(8,128)(2,1)} %get-tuple-element.189, bf16[32,3200]{1,0:T(8,128)(2,1)} %get-tuple-element.190), kind=kOutput, calls=%fused_computation | convolution fusion | flops 346112000 | bytes 42909696 | tf_op jit(solution)/shard_map/while/body/eval_jaxpr/cond/branch_1_fun/dot_general | solution.py:52
  701.4 9.3 conditional.4
  703.4 7.2 fusion.36
  711.4 1.3 collective-permute-start
  712.9 26.1 %all-reduce.4.cloned.1.call-done = bf16[32,1664]{1,0:T(8,128)(2,1)} async-done(((bf16[32,1664]{1,0:T(8,128)(2,1)}), bf16[32,1664]{1,0:T(8,128)(2,1)}) %all-reduce.4.cloned.1.call-update) | async-done | bytes 106512 | tf_op jit(solution)/shard_map/while/body/eval_jaxpr/psum | solution.py:120
  741.2 1.3 collective-permute-start.1
  742.5 17.3 %conditional.5 = (f32[1664,3200]{1,0:T(8,128)}) conditional(s32[]{:T(128)} %convert_element_type.179, f32[1664,3200]{1,0:T(8,128)} %get-tuple-element.404, (bf16[32,1664]{1,0:T(8,128)(2,1)}, bf16[32,3200]{1,0:T(8,128)(2,1)}, f32[1664,3200]{1,0:T(8,128)}) %tuple.68), branch_computations={%region_6.6_spmd, %region_7.7_spmd} | conditional | flops 346112000 | bytes 42909704 | solution.py:126
  742.5 17.3 %convolution_add_fusion = f32[1664,3200]{1,0:T(8,128)} fusion(f32[1664,3200]{1,0:T(8,128)} %get-tuple-element.188, bf16[32,1664]{1,0:T(8,128)(2,1)} %get-tuple-element.189, bf16[32,3200]{1,0:T(8,128)(2,1)} %get-tuple-element.190), kind=kOutput, calls=%fused_computation | convolution fusion | flops 346112000 | bytes 42909696 | tf_op jit(solution)/shard_map/while/body/eval_jaxpr/cond/branch_1_fun/dot_general | solution.py:52
  759.8 12.3 %convert_element_type.68 = bf16[1664,3200]{1,0:T(8,128)(2,1)} convert(f32[1664,3200]{1,0:T(8,128)} %get-tuple-element.215) | non-fusion elementwise | flops 5324800 | bytes 31948800 | tf_op jit(solution)/shard_map/convert_element_type | solution.py:140
  772.1 150.4 %fusion = bf16[64,3200]{1,0:T(8,128)(2,1)S(1)} fusion(bf16[1664,3200]{1,0:T(8,128)(2,1)} %convert_element_type.68), kind=kCustom, calls=%all-reduce-scatter | all-reduce-scatter fusion | flops 6553601 | bytes 11060224
  922.7 2.0 collective-permute-start.7
  925.9 1.9 collective-permute-start.2
  927.8 5.7 collective-permute-start.3
  933.5 1.9 collective-permute-start.4
  935.5 1.9 collective-permute-start.5
  937.4 11.5 %collective-permute-done.7 = bf16[52,3200]{1,0:T(8,128)(2,1)S(1)} collective-permute-done((bf16[52,3200]{1,0:T(8,128)(2,1)S(1)}, bf16[52,3200]{1,0:T(8,128)(2,1)S(1)}, u32[]{:S(2)}, u32[]{:S(2)}) %collective-permute-start.7) | collective-permute-done | bytes 332832
  948.9 1.9 collective-permute-start.6
  951.6 7.9 collective-permute-done.2
  959.5 1.4 collective-permute-done.3
  962.5 46.2 %collective-permute-done.6 = bf16[64,3200]{1,0:T(8,128)(2,1)} collective-permute-done((bf16[64,3200]{1,0:T(8,128)(2,1)S(1)}, bf16[64,3200]{1,0:T(8,128)(2,1)}, u32[]{:S(2)}, u32[]{:S(2)}) %collective-permute-start.6) | collective-permute-done | bytes 409632
  1008.7 21.1 %concatenate = bf16[436,3200]{1,0:T(8,128)(2,1)S(1)} concatenate(bf16[52,3200]{1,0:T(8,128)(2,1)} %copy-done.7, bf16[64,3200]{1,0:T(8,128)(2,1)} %collective-permute-done.6, bf16[64,3200]{1,0:T(8,128)(2,1)} %copy-done.6, bf16[64,3200]{1,0:T(8,128)(2,1)} %copy-done.5, bf16[64,3200]{1,0:T(8,128)(2,1)} %copy-done.4, bf16[64,3200]{1,0:T(8,128)(2,1)} %copy-done.3, ...), dimensions={0} | concatenate | bytes 5580800
  (193 shorter events, 54.2 us)
Async XLA Ops:
  13.1 9.6 copy-start.10
  13.1 9.7 copy-start.2
  13.1 9.7 copy-start.8
  13.1 273.4 %all-to-all-start = ((bf16[32,52,3200]{2,1,0:T(8,128)(2,1)}), bf16[32,52,3200]{2,1,0:T(8,128)(2,1)}, u32[]{:S(2)}, u32[]{:S(2)}) async-start(bf16[32,52,3200]{2,1,0:T(8,128)(2,1)} %stack.3), calls=%async_computation | async-start | bytes 22937600 | tf_op jit(solution)/shard_map/all_to_all | solution.py:71
  300.4 8.5 copy-start.1
  309.0 46.5 %all-reduce.4.cloned.1.call-start = ((), (), s32[]{:S(2)}) async-start(), calls=%async_computation.1 | async-start | bytes 212992 | tf_op jit(solution)/shard_map/while/body/eval_jaxpr/psum | solution.py:120
  313.7 0.6 copy-start
  314.4 44.6 %collective-permute-start = (bf16[32,3200]{1,0:T(8,128)(2,1)S(1)}, bf16[32,3200]{1,0:T(8,128)(2,1)S(1)}, u32[]{:S(2)}, u32[]{:S(2)}) collective-permute-start(bf16[32,3200]{1,0:T(8,128)(2,1)S(1)} %get-tuple-element.368), channel_id=1, source_target_pairs={{64,0},{128,64},{192,128},{65,1},{129,65},{193,129},{66,2},{130,66... | collective-permute-start | bytes 614408 | tf_op jit(solution)/shard_map/while/body/eval_jaxpr/ppermute | solution.py:22
  357.6 7.1 collective-permute-start.1
  364.7 54.4 %all-reduce.4.cloned.1.call-start = ((), (), s32[]{:S(2)}) async-start(), calls=%async_computation.1 | async-start | bytes 212992 | tf_op jit(solution)/shard_map/while/body/eval_jaxpr/psum | solution.py:120
  369.4 0.6 copy-start
  370.0 52.5 %collective-permute-start = (bf16[32,3200]{1,0:T(8,128)(2,1)S(1)}, bf16[32,3200]{1,0:T(8,128)(2,1)S(1)}, u32[]{:S(2)}, u32[]{:S(2)}) collective-permute-start(bf16[32,3200]{1,0:T(8,128)(2,1)S(1)} %get-tuple-element.368), channel_id=1, source_target_pairs={{64,0},{128,64},{192,128},{65,1},{129,65},{193,129},{66,2},{130,66... | collective-permute-start | bytes 614408 | tf_op jit(solution)/shard_map/while/body/eval_jaxpr/ppermute | solution.py:22
  421.2 7.1 collective-permute-start.1
  428.3 56.1 %all-reduce.4.cloned.1.call-start = ((), (), s32[]{:S(2)}) async-start(), calls=%async_computation.1 | async-start | bytes 212992 | tf_op jit(solution)/shard_map/while/body/eval_jaxpr/psum | solution.py:120
  433.0 0.6 copy-start
  433.6 54.3 %collective-permute-start = (bf16[32,3200]{1,0:T(8,128)(2,1)S(1)}, bf16[32,3200]{1,0:T(8,128)(2,1)S(1)}, u32[]{:S(2)}, u32[]{:S(2)}) collective-permute-start(bf16[32,3200]{1,0:T(8,128)(2,1)S(1)} %get-tuple-element.368), channel_id=1, source_target_pairs={{64,0},{128,64},{192,128},{65,1},{129,65},{193,129},{66,2},{130,66... | collective-permute-start | bytes 614408 | tf_op jit(solution)/shard_map/while/body/eval_jaxpr/ppermute | solution.py:22
  486.6 7.1 collective-permute-start.1
  493.7 56.1 %all-reduce.4.cloned.1.call-start = ((), (), s32[]{:S(2)}) async-start(), calls=%async_computation.1 | async-start | bytes 212992 | tf_op jit(solution)/shard_map/while/body/eval_jaxpr/psum | solution.py:120
  506.3 0.6 copy-start
  507.0 63.7 %collective-permute-start = (bf16[32,3200]{1,0:T(8,128)(2,1)S(1)}, bf16[32,3200]{1,0:T(8,128)(2,1)S(1)}, u32[]{:S(2)}, u32[]{:S(2)}) collective-permute-start(bf16[32,3200]{1,0:T(8,128)(2,1)S(1)} %get-tuple-element.368), channel_id=1, source_target_pairs={{64,0},{128,64},{192,128},{65,1},{129,65},{193,129},{66,2},{130,66... | collective-permute-start | bytes 614408 | tf_op jit(solution)/shard_map/while/body/eval_jaxpr/ppermute | solution.py:22
  552.0 18.6 %collective-permute-start.1 = (bf16[32,1664]{1,0:T(8,128)(2,1)S(1)}, bf16[32,1664]{1,0:T(8,128)(2,1)S(1)}, u32[]{:S(2)}, u32[]{:S(2)}) collective-permute-start(bf16[32,1664]{1,0:T(8,128)(2,1)S(1)} %get-tuple-element.369), channel_id=1, source_target_pairs={{64,0},{128,64},{192,128},{65,1},{129,65},{193,129},{66,2},{130,66... | collective-permute-start | bytes 319496 | tf_op jit(solution)/shard_map/while/body/eval_jaxpr/ppermute | solution.py:22
  570.6 44.6 %all-reduce.4.cloned.1.call-start = ((), (), s32[]{:S(2)}) async-start(), calls=%async_computation.1 | async-start | bytes 212992 | tf_op jit(solution)/shard_map/while/body/eval_jaxpr/psum | solution.py:120
  583.3 0.6 copy-start
  583.9 52.1 %collective-permute-start = (bf16[32,3200]{1,0:T(8,128)(2,1)S(1)}, bf16[32,3200]{1,0:T(8,128)(2,1)S(1)}, u32[]{:S(2)}, u32[]{:S(2)}) collective-permute-start(bf16[32,3200]{1,0:T(8,128)(2,1)S(1)} %get-tuple-element.368), channel_id=1, source_target_pairs={{64,0},{128,64},{192,128},{65,1},{129,65},{193,129},{66,2},{130,66... | collective-permute-start | bytes 614408 | tf_op jit(solution)/shard_map/while/body/eval_jaxpr/ppermute | solution.py:22
  617.4 18.6 %collective-permute-start.1 = (bf16[32,1664]{1,0:T(8,128)(2,1)S(1)}, bf16[32,1664]{1,0:T(8,128)(2,1)S(1)}, u32[]{:S(2)}, u32[]{:S(2)}) collective-permute-start(bf16[32,1664]{1,0:T(8,128)(2,1)S(1)} %get-tuple-element.369), channel_id=1, source_target_pairs={{64,0},{128,64},{192,128},{65,1},{129,65},{193,129},{66,2},{130,66... | collective-permute-start | bytes 319496 | tf_op jit(solution)/shard_map/while/body/eval_jaxpr/ppermute | solution.py:22
  636.0 41.2 %all-reduce.4.cloned.1.call-start = ((), (), s32[]{:S(2)}) async-start(), calls=%async_computation.1 | async-start | bytes 212992 | tf_op jit(solution)/shard_map/while/body/eval_jaxpr/psum | solution.py:120
  648.7 0.6 copy-start
  649.3 48.7 %collective-permute-start = (bf16[32,3200]{1,0:T(8,128)(2,1)S(1)}, bf16[32,3200]{1,0:T(8,128)(2,1)S(1)}, u32[]{:S(2)}, u32[]{:S(2)}) collective-permute-start(bf16[32,3200]{1,0:T(8,128)(2,1)S(1)} %get-tuple-element.368), channel_id=1, source_target_pairs={{64,0},{128,64},{192,128},{65,1},{129,65},{193,129},{66,2},{130,66... | collective-permute-start | bytes 614408 | tf_op jit(solution)/shard_map/while/body/eval_jaxpr/ppermute | solution.py:22
  679.5 18.6 %collective-permute-start.1 = (bf16[32,1664]{1,0:T(8,128)(2,1)S(1)}, bf16[32,1664]{1,0:T(8,128)(2,1)S(1)}, u32[]{:S(2)}, u32[]{:S(2)}) collective-permute-start(bf16[32,1664]{1,0:T(8,128)(2,1)S(1)} %get-tuple-element.369), channel_id=1, source_target_pairs={{64,0},{128,64},{192,128},{65,1},{129,65},{193,129},{66,2},{130,66... | collective-permute-start | bytes 319496 | tf_op jit(solution)/shard_map/while/body/eval_jaxpr/ppermute | solution.py:22
  698.1 41.0 %all-reduce.4.cloned.1.call-start = ((), (), s32[]{:S(2)}) async-start(), calls=%async_computation.1 | async-start | bytes 212992 | tf_op jit(solution)/shard_map/while/body/eval_jaxpr/psum | solution.py:120
  710.7 0.6 copy-start
  711.4 48.5 %collective-permute-start = (bf16[32,3200]{1,0:T(8,128)(2,1)S(1)}, bf16[32,3200]{1,0:T(8,128)(2,1)S(1)}, u32[]{:S(2)}, u32[]{:S(2)}) collective-permute-start(bf16[32,3200]{1,0:T(8,128)(2,1)S(1)} %get-tuple-element.368), channel_id=1, source_target_pairs={{64,0},{128,64},{192,128},{65,1},{129,65},{193,129},{66,2},{130,66... | collective-permute-start | bytes 614408 | tf_op jit(solution)/shard_map/while/body/eval_jaxpr/ppermute | solution.py:22
  741.2 18.6 %collective-permute-start.1 = (bf16[32,1664]{1,0:T(8,128)(2,1)S(1)}, bf16[32,1664]{1,0:T(8,128)(2,1)S(1)}, u32[]{:S(2)}, u32[]{:S(2)}) collective-permute-start(bf16[32,1664]{1,0:T(8,128)(2,1)S(1)} %get-tuple-element.369), channel_id=1, source_target_pairs={{64,0},{128,64},{192,128},{65,1},{129,65},{193,129},{66,2},{130,66... | collective-permute-start | bytes 319496 | tf_op jit(solution)/shard_map/while/body/eval_jaxpr/ppermute | solution.py:22
  772.1 152.5 %copy-start.9 = (u32[256]{0:T(256)S(1)}, u32[256]{0:T(256)}, u32[]{:S(2)}) copy-start(u32[256]{0:T(256)} %constant.123) | copy-start | bytes 3076
  922.7 26.2 %collective-permute-start.7 = (bf16[52,3200]{1,0:T(8,128)(2,1)S(1)}, bf16[52,3200]{1,0:T(8,128)(2,1)S(1)}, u32[]{:S(2)}, u32[]{:S(2)}) collective-permute-start(bf16[52,3200]{1,0:T(8,128)(2,1)S(1)} %slice.4), channel_id=1, source_target_pairs={{0,12},{2,14},{4,16},{6,18},{8,20},{10,22},{12,24},{14,26},{16,28}... | collective-permute-start | bytes 998408
  925.9 33.6 %collective-permute-start.2 = (bf16[64,3200]{1,0:T(8,128)(2,1)S(1)}, bf16[64,3200]{1,0:T(8,128)(2,1)S(1)}, u32[]{:S(2)}, u32[]{:S(2)}) collective-permute-start(bf16[64,3200]{1,0:T(8,128)(2,1)S(1)} %fusion), channel_id=1, source_target_pairs={{0,2},{2,4},{4,6},{6,8},{8,10},{10,12},{12,14},{14,16},{16,18},{18... | collective-permute-start | bytes 1228808
  927.8 33.1 %collective-permute-start.3 = (bf16[64,3200]{1,0:T(8,128)(2,1)S(1)}, bf16[64,3200]{1,0:T(8,128)(2,1)S(1)}, u32[]{:S(2)}, u32[]{:S(2)}) collective-permute-start(bf16[64,3200]{1,0:T(8,128)(2,1)S(1)} %fusion), channel_id=1, source_target_pairs={{0,4},{2,6},{4,8},{6,10},{8,12},{10,14},{12,16},{14,18},{16,20},{1... | collective-permute-start | bytes 1228808
  933.5 27.3 %collective-permute-start.4 = (bf16[64,3200]{1,0:T(8,128)(2,1)S(1)}, bf16[64,3200]{1,0:T(8,128)(2,1)S(1)}, u32[]{:S(2)}, u32[]{:S(2)}) collective-permute-start(bf16[64,3200]{1,0:T(8,128)(2,1)S(1)} %fusion), channel_id=1, source_target_pairs={{0,6},{2,8},{4,10},{6,12},{8,14},{10,16},{12,18},{14,20},{16,22},{... | collective-permute-start | bytes 1228808
  935.5 25.4 %collective-permute-start.5 = (bf16[64,3200]{1,0:T(8,128)(2,1)S(1)}, bf16[64,3200]{1,0:T(8,128)(2,1)S(1)}, u32[]{:S(2)}, u32[]{:S(2)}) collective-permute-start(bf16[64,3200]{1,0:T(8,128)(2,1)S(1)} %fusion), channel_id=1, source_target_pairs={{0,8},{2,10},{4,12},{6,14},{8,16},{10,18},{12,20},{14,22},{16,24},... | collective-permute-start | bytes 1228808
  948.9 12.0 %copy-start.7 = (bf16[52,3200]{1,0:T(8,128)(2,1)}, bf16[52,3200]{1,0:T(8,128)(2,1)S(1)}, u32[]{:S(2)}) copy-start(bf16[52,3200]{1,0:T(8,128)(2,1)S(1)} %collective-permute-done.7) | copy-start | bytes 998404
  948.9 59.8 %collective-permute-start.6 = (bf16[64,3200]{1,0:T(8,128)(2,1)S(1)}, bf16[64,3200]{1,0:T(8,128)(2,1)}, u32[]{:S(2)}, u32[]{:S(2)}) collective-permute-start(bf16[64,3200]{1,0:T(8,128)(2,1)S(1)} %fusion), channel_id=1, source_target_pairs={{0,10},{2,12},{4,14},{6,16},{8,18},{10,20},{12,22},{14,24},{16,26}... | collective-permute-start | bytes 1228808
  959.5 1.4 copy-start.3
  960.9 0.8 copy-start.4
  960.9 0.9 copy-start.5
  961.8 0.8 copy-start.6
Sparse Core Ops, SparseCore 0:
  314.5 40.8 all-reduce.3
  370.1 48.8 all-reduce.3
  433.8 50.6 all-reduce.3
  507.1 42.6 all-reduce.3
  584.1 31.1 all-reduce.3
  649.5 27.7 all-reduce.3
  711.5 27.4 all-reduce.3
